TPU v7x, 256 devices: a whole 4x4x8 slice. The times are simulated.
256 devices in a mesh: heads: 8 (over y, x_lo), ctx: 32 (over z, x_hi, core).
Axes of the slice: x: 4 (x_hi: 2, x_lo: 2; x = x_hi * 2 + x_lo), y: 4, z: 8, core: 2. Of those that a mesh axis runs over, the one named last changes fastest.
Arguments:
- query: float32 [4096, 8192], P('ctx', 'heads'), parts along dimension 1, may hold values from -6 to 6
- key: float32 [4096, 1024], P('ctx', 'heads'), parts along dimension 1, may hold values from -6 to 6
- value: float32 [4096, 1024], P('ctx', 'heads'), parts along dimension 1, may hold values from -6 to 6
- output: float32 [4096, 8192], P('ctx', 'heads'), parts along dimension 1, may hold values from -6 to 6
- grad_output: float32 [4096, 8192], P('ctx', 'heads'), parts along dimension 1, may hold values from -6 to 6
- lse: float32 [64, 4096], P('heads', 'ctx'), parts along dimension 0, may hold values from -0.5 to 20, as said below
- span_order: int32 [512], P('heads'), parts along dimension 0, may hold values from 0 to 63, as said below
Outputs:
- grad_query: float32 [4096, 8192], P('ctx', 'heads'), parts along dimension 1
- grad_key: float32 [4096, 1024], P('ctx', 'heads'), parts along dimension 1
- grad_value: float32 [4096, 1024], P('ctx', 'heads'), parts along dimension 1
There are 8 independent parts, one for each index of `heads`. A program takes and returns all parts, laid end to end along the dimension named above; each array names one. Nothing has to cross between parts.
Inputs may be any that keep to these rules, and one draw needn't show every extreme that they name: `span_order`: a permutation: each of 0 to 63 once. `lse`: log of the row's causal key count, plus 0.5, plus a perturbation.
All inputs are finite; a program needn't handle non-finite values.
Results may differ from a plain program's by a relative error of at most 0.0003.
Values sent between devices are 32-bit elements; how exact they have to be, the bound alone decides.
No kernel may reach another device: no remote copies, remote signals or barrier semaphores. Data moves between devices by JAX's collectives and lax.ppermute only.
A program may use at most 64 MiB of HBM per device.

v0:
```python
import math

import jax
import jax.numpy as jnp
from jax import lax
from jax.sharding import PartitionSpec as P


def positions(order, first, count, half):
    rows = first + jnp.arange(count, dtype=jnp.int32)
    slots = rows // half
    hits = slots[:, None] == jnp.arange(order.shape[0], dtype=jnp.int32)[None, :]
    base = jnp.sum(jnp.where(hits, order[None, :], 0), axis=1)
    return base * half + rows % half


def tile_grads(qheads, dout, lse_rows, delta, qpos, kblock, vblock, kpos, scale):
    highest = lax.Precision.HIGHEST
    scores = jnp.einsum("qhd,kd->hqk", qheads, kblock, precision=highest) * scale
    visible = kpos[None, :] <= qpos[:, None]
    prob = jnp.exp(jnp.where(visible[None], scores - lse_rows[:, :, None], -1e30))
    dprob = jnp.einsum("qhd,kd->hqk", dout, vblock, precision=highest)
    dscore = prob * (dprob - delta[:, :, None])
    grad_q = jnp.einsum("hqk,kd->qhd", dscore, kblock, precision=highest) * scale
    grad_k = jnp.einsum("hqk,qhd->kd", dscore, qheads, precision=highest) * scale
    grad_v = jnp.einsum("hqk,qhd->kd", prob, dout, precision=highest)
    return (grad_q, grad_k, grad_v)


def local(query, key, value, output, grad_output, lse, span_order):
    count, width = key.shape
    heads = lse.shape[0]
    half = count // 2
    scale = 1.0 / math.sqrt(width)
    rank = lax.axis_index("ctx")
    qpos = positions(span_order, rank * count, count, half)
    qheads = query.reshape(count, heads, width)
    dout = grad_output.reshape(count, heads, width)
    oheads = output.reshape(count, heads, width)
    delta = jnp.sum(dout * oheads, axis=2).T

    def full_block(kblock, vblock, kpos):
        return tile_grads(qheads, dout, lse, delta, qpos, kblock, vblock, kpos, scale)

    def block_grads(kblock, vblock, kpos):
        return full_block(kblock, vblock, kpos)

    acc_q = jnp.zeros((count, heads, width), jnp.float32)
    kpiece = lax.all_gather(key, "ctx", axis=0, tiled=True)
    rows = kpiece.shape[0]
    step = math.gcd(rows, count)
    kparts = kpiece.reshape(rows // step, step, width)
    vparts = lax.all_gather(value, "ctx", axis=0, tiled=True).reshape(rows // step, step, width)

    def inner(acc_q, item):
        kblock, vblock, index = item
        kpos = positions(span_order, index * step, step, half)
        grad_q, grad_k, grad_v = block_grads(kblock, vblock, kpos)
        return (acc_q + grad_q, (grad_k, grad_v))

    start_q = jnp.zeros((count, heads, width), jnp.float32)
    indices = jnp.arange(rows // step, dtype=jnp.int32)
    acc_q, (kgrads, vgrads) = lax.scan(inner, start_q, (kparts, vparts, indices))
    grad_q = acc_q
    grad_k = kgrads.reshape(rows, width)
    grad_v = vgrads.reshape(rows, width)
    kterms = grad_k
    vterms = grad_v
    acc_q, kterms, vterms = (grad_q, kterms, vterms)
    grad_key, grad_value = (
        lax.psum_scatter(kterms, "ctx", scatter_dimension=0, tiled=True),
        lax.psum_scatter(vterms, "ctx", scatter_dimension=0, tiled=True),
    )
    return (acc_q.reshape(count, heads * width), grad_key, grad_value)


def solution(mesh):
    in_specs = (
        P("ctx", "heads"),
        P("ctx", "heads"),
        P("ctx", "heads"),
        P("ctx", "heads"),
        P("ctx", "heads"),
        P("heads", "ctx"),
        P("heads"),
    )
    out_specs = (P("ctx", "heads"), P("ctx", "heads"), P("ctx", "heads"))
    return jax.shard_map(local, mesh=mesh, in_specs=in_specs, out_specs=out_specs, check_vma=False)
```

profile of v0, /device:TPU:8, one launch (start us, length us, event | category | flops | bytes accessed | tf_op | source)
XLA Modules:
  0.0 689.7 jit_solution(1414955238921803853)
XLA Ops:
  11.1 82.5 %all-gather.3.cloned.1.call-done = f32[4096,128]{1,0:T(8,128)} async-done(((f32[128,128]{1,0:T(8,128)}), f32[4096,128]{1,0:T(8,128)}) %all-gather.3.cloned.1.call-update) | async-done | bytes 2097168 | tf_op jit(solution)/shard_map/all_gather | solution.py:49
  93.6 79.4 %all-gather.5.cloned.1.call-done = f32[4096,128]{1,0:T(8,128)} async-done(((f32[128,128]{1,0:T(8,128)}), f32[4096,128]{1,0:T(8,128)}) %all-gather.5.cloned.1.call-update) | async-done | bytes 2097168 | tf_op jit(solution)/shard_map/all_gather | solution.py:53
  173.0 271.6 %while.17 = (s32[]{:T(128)}, f32[128,8,128]{0,2,1:T(8,128)S(1)}, f32[32,128,128]{2,1,0:T(8,128)}, f32[32,128,128]{2,1,0:T(8,128)}, f32[32,128,128]{2,1,0:T(8,128...) while((s32[]{:T(128)}, f32[128,8,128]{0,2,1:T(8,128)S(1)}, ...), condition=%wide.region_4.5_spmd.clone, body=%wide.region_2.4_spmd.clone.sunk | while | flops 1007742592 | bytes 6664155 | solution.py:63
  174.5 1.5 fusion.57
  177.4 1.5 fusion.59
  185.9 1.5 fusion.59
  191.4 1.5 fusion.57
  194.4 1.5 fusion.59
  202.9 1.5 fusion.59
  211.4 1.5 fusion.59
  216.9 1.5 fusion.57
  219.8 1.5 fusion.59
  228.3 1.5 fusion.59
  236.8 1.5 fusion.59
  245.3 1.5 fusion.59
  253.8 1.5 fusion.59
  259.3 1.5 fusion.57
  262.3 1.5 fusion.59
  267.8 1.5 fusion.57
  270.8 1.5 fusion.59
  276.3 1.5 fusion.57
  279.2 1.5 fusion.59
  287.7 1.5 fusion.59
  293.3 1.5 fusion.57
  296.2 1.5 fusion.59
  304.7 1.5 fusion.59
  310.2 1.5 fusion.57
  313.2 1.5 fusion.59
  318.7 1.5 fusion.57
  321.7 1.5 fusion.59
  330.1 1.5 fusion.59
  335.7 1.5 fusion.57
  338.6 1.5 fusion.59
  347.1 1.5 fusion.59
  355.6 1.5 fusion.59
  364.1 1.5 fusion.59
  372.6 1.5 fusion.59
  378.1 1.5 fusion.57
  381.1 1.5 fusion.59
  389.6 1.5 fusion.59
  398.1 1.5 fusion.59
  406.5 1.5 fusion.59
  415.0 1.5 fusion.59
  423.5 1.5 fusion.59
  432.0 1.5 fusion.59
  440.5 1.5 fusion.59
  446.2 114.5 %reduce-scatter.5.cloned.1.call-done = f32[128,128]{1,0:T(8,128)} async-done(((f32[4096,128]{1,0:T(8,128)}), f32[128,128]{1,0:T(8,128)}) %reduce-scatter.5.cloned.1.call-update) | async-done | bytes 65552 | tf_op jit(solution)/shard_map/reduce_scatter | solution.py:72
  560.7 122.5 %reduce-scatter.3.cloned.1.call-done = f32[128,128]{1,0:T(8,128)} async-done(((f32[4096,128]{1,0:T(8,128)}), f32[128,128]{1,0:T(8,128)}) %reduce-scatter.3.cloned.1.call-update) | async-done | bytes 65552 | tf_op jit(solution)/shard_map/reduce_scatter | solution.py:71
  (307 shorter events, 189.2 us)
Async XLA Ops:
  7.2 3.1 copy-start
  7.2 86.5 %all-gather.3.cloned.1.call-start = ((), (), s32[]{:S(2)}) async-start(), calls=%async_computation.2 | async-start | bytes 2162688 | tf_op jit(solution)/shard_map/all_gather | solution.py:49
  7.9 165.1 %all-gather.5.cloned.1.call-start = ((), (), s32[]{:S(2)}) async-start(), calls=%async_computation.3 | async-start | bytes 2162688 | tf_op jit(solution)/shard_map/all_gather | solution.py:53
  8.7 552.0 %reduce-scatter.5.cloned.1.call-start = ((), (), s32[]{:S(2)}) async-start(), calls=%async_computation.5 | async-start | bytes 2162688 | tf_op jit(solution)/shard_map/reduce_scatter | solution.py:72
  8.7 2.0 copy-start.1
  10.0 0.9 copy-start.3
  10.3 162.8 %copy-start.2 = (f32[8,128]{1,0:T(8,128)S(1)}, f32[8,128]{1,0:T(8,128)}, u32[]{:S(2)}) copy-start(f32[8,128]{1,0:T(8,128)} %param.14) | copy-start | bytes 12292
  444.6 238.6 %reduce-scatter.3.cloned.1.call-start = ((), (), s32[]{:S(2)}) async-start(), calls=%async_computation.4 | async-start | bytes 2162688 | tf_op jit(solution)/shard_map/reduce_scatter | solution.py:71
Sparse Core Ops, SparseCore 0:
  10.8 82.8 all-gather.2
  96.4 76.5 all-gather.4
  444.8 115.8 reduce-scatter.4
  565.8 117.3 reduce-scatter.2
where the time goes:
time: 695 us; the launch traced here: 690 us
  waiting for transfers between devices  401 us (58%)
  matrix products  224 us (32%)
  loops' own time  22.1 us (3%)
  local copies, waits for them, and re-layouts  21.7 us (3%)
  between operations  13.9 us (2%)
    reduce_scatter x1, waiting for transfers between devices, local(): lax.psum_scatter(kterms, 'ctx', scatter_dimension=0, tiled=True)  123 us
    reduce_scatter x1, waiting for transfers between devices, local(): lax.psum_scatter(vterms, 'ctx', scatter_dimension=0, tiled=True)  114 us
    all_gather x1, waiting for transfers between devices, local(): kpiece = lax.all_gather(key, 'ctx', axis=0, tiled=True)  82.5 us
    all_gather x1, waiting for transfers between devices, local(): lax.all_gather(value, 'ctx', axis=0, tiled=True)  79.4 us
    dot_general x32, matrix products, tile_grads(): jnp.einsum('hqk,kd->qhd', dscore, kblock, precision=highest) * scale  49.2 us
    dot_general x32, matrix products, tile_grads(): jnp.einsum('qhd,kd->hqk', qheads, kblock, precision=highest) * scale  47.7 us
    dot_general x32, matrix products, tile_grads(): dprob = jnp.einsum('qhd,kd->hqk', dout, vblock, precision=highest)  45.7 us
    dot_general x32, matrix products, tile_grads(): jnp.einsum('hqk,qhd->kd', dscore, qheads, precision=highest) * scale  40.9 us
  transfers between devices with their start and end apart: 4, of which 4 were waited for; matrix products, arithmetic and copies ran while one was open for 0% of the time, Pallas kernels for 0%

commit v1 on v0

v1 whole, which is shorter than its diff:
```python
import functools
import math

import jax
import jax.numpy as jnp
from jax import lax
from jax.experimental import pallas as pl
from jax.experimental.pallas import tpu as pltpu
from jax.sharding import PartitionSpec as P

ZS = 8
DH = 128
HQ = 8
LOG2E = 1.4426950408889634
BIG = 1e30
F32 = jnp.float32
BF16 = jnp.bfloat16
NT = (((1,), (1,)), ((), ()))
NN = (((1,), (0,)), ((), ()))
TN = (((0,), (0,)), ((), ()))


def send(x, dz=0, dx=0, dc=0):
    perm = []
    for z in range(ZS):
        for xh in range(2):
            for c in range(2):
                to = ((z + dz) % ZS) * 4 + ((xh + dx) % 2) * 2 + (c + dc) % 2
                perm.append((z * 4 + xh * 2 + c, to))
    return lax.ppermute(x, "ctx", perm)


def split(x):
    hi = x.astype(BF16)
    return hi, (x - hi.astype(F32)).astype(BF16)


def dot(a, b, dims=NN):
    return lax.dot_general(a, b, dims, preferred_element_type=F32)


def pack_kernel(q_ref, do_ref, o_ref, lse_ref, out_ref):
    out_ref[:, : HQ * DH] = q_ref[...]
    out_ref[:, HQ * DH : 2 * HQ * DH] = do_ref[...]
    rows = q_ref.shape[0]
    lane = lax.broadcasted_iota(jnp.int32, (rows, DH), 1)
    pad = jnp.zeros((DH - HQ, rows), F32)
    extra = jnp.concatenate([lse_ref[...] * (-LOG2E), pad], axis=0).T
    for h in range(HQ):
        s = slice(h * DH, (h + 1) * DH)
        delta = jnp.sum(do_ref[:, s] * o_ref[:, s], axis=1, keepdims=True)
        extra = jnp.where(lane == HQ + h, -delta, extra)
    out_ref[:, 2 * HQ * DH :] = extra


def grads_kernel(offsets, groups, diag, n_kv, has_dq, has_dkv, *refs):
    rank_ref, order_ref, *refs = refs
    nq, nk = len(groups), len(offsets)
    q_refs, do_refs, x_refs = refs[:nq], refs[nq : 2 * nq], refs[2 * nq : 3 * nq]
    refs = refs[3 * nq :]
    kv_refs, refs = refs[:n_kv], refs[n_kv:]
    dq_in, refs = (refs[:nq], refs[nq:]) if has_dq else (None, refs)
    dkv_in, refs = (refs[:nk], refs[nk:]) if has_dkv else (None, refs)
    dq_out, dkv_out, refs = refs[:nq], refs[nq : nq + nk], refs[nq + nk :]
    kc, vc, qc, dc = refs
    h = pl.program_id(0)
    half = DH // 2
    rank = rank_ref[0]
    z, line = rank // 4, rank % 4
    lane = lax.broadcasted_iota(jnp.int32, (half, DH), 1)

    @pl.when(h == 0)
    def _():
        halves = []
        for ref in kv_refs:
            for i in range(ref.shape[0] // half):
                halves.append((ref, i * half))
        for i, (ref, first) in enumerate(halves):
            owner = lax.rem(z + (offsets[i // 2] + ZS), ZS) * 4 + line
            pos = order_ref[owner * 2 + i % 2]
            hot = jnp.where((lane == pos) | ((lane >= 64) & (lane < 67)), 1.0, 0.0).astype(BF16)
            to = slice(i * half, (i + 1) * half)
            hi, lo = split(ref[first : first + half, :DH])
            kc[to, :] = jnp.concatenate([hi, lo, hi, hot], axis=1)
            hi, lo = split(ref[first : first + half, DH:])
            vc[to, :] = jnp.concatenate([hi, lo, hi, hot], axis=1)
        for i in range(nk):
            if has_dkv:
                dkv_out[i][...] = dkv_in[i][...]
            else:
                dkv_out[i][...] = jnp.zeros_like(dkv_out[i])

    for g, (dx, dcore) in enumerate(groups):
        peer = z * 4 + lax.bitwise_xor(line, dx * 2 + dcore)
        for j in range(2):
            s = slice(j * half, (j + 1) * half)
            to = slice(g * DH + j * half, g * DH + (j + 1) * half)
            x = x_refs[g][s, :]
            pos = order_ref[peer * 2 + j]

            def terms(column):
                c = jnp.sum(jnp.where(lane == column, x, 0.0), axis=1, keepdims=True)
                a = c.astype(BF16).astype(F32)
                b = (c - a).astype(BF16).astype(F32)
                d = c - a - b
                return jnp.where(lane == 64, a, jnp.where(lane == 65, b, jnp.where(lane == 66, d, 0.0)))

            bias = jnp.where((lane < 64) & (lane > pos), -BIG, terms(h)).astype(BF16)
            hi, lo = split(q_refs[g][s, :] * (LOG2E / math.sqrt(DH)))
            qc[to, :] = jnp.concatenate([hi, hi, lo, bias], axis=1)
            bias = terms(h + HQ).astype(BF16)
            hi, lo = split(do_refs[g][s, :])
            dc[to, :] = jnp.concatenate([hi, hi, lo, bias], axis=1)

    p = jnp.exp2(dot(kc[...], qc[...], NT))
    if diag:
        a = lax.broadcasted_iota(jnp.int32, p.shape, 0)
        b = lax.broadcasted_iota(jnp.int32, p.shape, 1)
        later = (a < DH) & (b < DH) & (a // half == b // half) & (a > b)
        p = jnp.where(later, 0.0, p)
    ds = p * dot(vc[...], dc[...], NT)
    p_hi, p_lo = split(p)
    r = dot(p_hi, dc[:, DH : 3 * DH])
    dv = r[:, :DH] + r[:, DH:] + dot(p_lo, dc[:, :DH])
    ds_hi, ds_lo = split(ds)
    r = dot(ds_hi, qc[:, DH : 3 * DH])
    dk = (r[:, :DH] + r[:, DH:] + dot(ds_lo, qc[:, :DH])) * (1.0 / LOG2E)
    for i in range(nk):
        s = slice(i * DH, (i + 1) * DH)
        dkv_out[i][:, :DH] += dk[s]
        dkv_out[i][:, DH:] += dv[s]
    r = dot(ds_hi, kc[:, : 2 * DH], TN)
    dq = (r[:, :DH] + r[:, DH:] + dot(ds_lo, kc[:, :DH], TN)) * (1.0 / math.sqrt(DH))
    for g in range(nq):
        t = dq[g * DH : (g + 1) * DH]
        dq_out[g][...] = dq_in[g][...] + t if has_dq else t


def grads(rank, order, packs, groups, blocks, dq=None, dkv=None):
    offsets = list(blocks)
    pieces = [piece for o in offsets for piece in blocks[o]]
    nq, nk = len(packs), len(offsets)
    rows = packs[0].shape[0]
    whole = lambda a: pl.BlockSpec(a.shape, lambda h: (0, 0))
    head = lambda first: pl.BlockSpec((rows, DH), lambda h: (0, first + h))
    scalar = pl.BlockSpec(memory_space=pltpu.SMEM)
    in_specs = [scalar, scalar]
    in_specs += [head(0)] * nq + [head(HQ)] * nq + [pl.BlockSpec((rows, DH), lambda h: (0, 2 * HQ))] * nq
    in_specs += [whole(p) for p in pieces]
    args = [rank, order, *packs, *packs, *packs, *pieces]
    aliases = {}
    if dq is not None:
        for g in range(nq):
            aliases[len(args) + g] = g
        in_specs += [head(0)] * nq
        args += dq
    if dkv is not None:
        for i in range(nk):
            aliases[len(args) + i] = nq + i
        in_specs += [pl.BlockSpec((rows, 2 * DH), lambda h: (0, 0))] * nk
        args += [dkv[o] for o in offsets]
    out_specs = [head(0)] * nq + [pl.BlockSpec((rows, 2 * DH), lambda h: (0, 0))] * nk
    out_shape = [jax.ShapeDtypeStruct((rows, HQ * DH), F32)] * nq + [jax.ShapeDtypeStruct((rows, 2 * DH), F32)] * nk
    keys, queries = nk * rows, nq * rows
    diag = 0 in offsets and groups[0] == (0, 0)
    outs = pl.pallas_call(
        functools.partial(grads_kernel, offsets, groups, diag, len(pieces), dq is not None, dkv is not None),
        grid=(HQ,),
        in_specs=in_specs,
        out_specs=out_specs,
        out_shape=out_shape,
        input_output_aliases=aliases,
        scratch_shapes=[pltpu.VMEM((keys, 4 * DH), BF16)] * 2 + [pltpu.VMEM((queries, 4 * DH), BF16)] * 2,
        compiler_params=pltpu.CompilerParams(vmem_limit_bytes=40 * 2**20),
        cost_estimate=pl.CostEstimate(
            flops=HQ * keys * queries * DH * 2 * 20, bytes_accessed=2**21, transcendentals=HQ * keys * queries
        ),
        name="grads",
    )(*args)
    return outs[:nq], dict(zip(offsets, outs[nq:]))


def local(query, key, value, output, grad_output, lse, span_order):
    rows = key.shape[0]
    rank = lax.axis_index("ctx").astype(jnp.int32).reshape(1)
    pack = pl.pallas_call(
        pack_kernel,
        out_shape=jax.ShapeDtypeStruct((rows, (2 * HQ + 1) * DH), F32),
        compiler_params=pltpu.CompilerParams(vmem_limit_bytes=32 * 2**20),
        name="pack",
    )(query, grad_output, output, lse)
    kv = jnp.concatenate([key, value], axis=1)
    half = rows // 2

    pack_x = send(pack, dx=1)
    pack_c = send(pack, dc=1)
    f1, b1 = send(kv, dz=1), send(kv, dz=-1)
    f2, b2 = send(f1, dz=1), send(b1, dz=-1)
    f3, b3 = send(f2, dz=1), send(b2, dz=-1)
    f4, b4 = send(f3[:half], dz=1), send(b3[half:], dz=-1)
    pack_xc = send(pack_x, dc=1)
    near = {0: [kv], -1: [f1], 1: [b1], -2: [f2], 2: [b2]}
    far = {-3: [f3], 3: [b3], 4: [f4, b4]}
    own, other = [(0, 0), (0, 1)], [(1, 0), (1, 1)]

    dq_own, dkv_near = grads(rank, span_order, [pack, pack_c], own, near)
    dq_own, dkv_far = grads(rank, span_order, [pack, pack_c], own, far, dq=dq_own)
    dq_other, dkv_far = grads(rank, span_order, [pack_x, pack_xc], other, far, dkv=dkv_far)
    dq_other, dkv_near = grads(rank, span_order, [pack_x, pack_xc], other, near, dq=dq_other, dkv=dkv_near)

    f, b = send(dkv_far[4][:half], dz=1), send(dkv_far[4][half:], dz=-1)
    f = send(dkv_far[3].at[:half].add(f), dz=1)
    b = send(dkv_far[-3].at[half:].add(b), dz=-1)
    f, b = send(f + dkv_near[2], dz=1), send(b + dkv_near[-2], dz=-1)
    f, b = send(f + dkv_near[1], dz=1), send(b + dkv_near[-1], dz=-1)
    dkv = dkv_near[0] + f + b

    dq = dq_own[0] + send(dq_own[1], dc=1)
    dq = dq + send(dq_other[0] + send(dq_other[1], dc=1), dx=1)
    return dq, dkv[:, :DH], dkv[:, DH:]


def solution(mesh):
    in_specs = (
        P("ctx", "heads"),
        P("ctx", "heads"),
        P("ctx", "heads"),
        P("ctx", "heads"),
        P("ctx", "heads"),
        P("heads", "ctx"),
        P("heads"),
    )
    out_specs = (P("ctx", "heads"), P("ctx", "heads"), P("ctx", "heads"))
    return jax.shard_map(local, mesh=mesh, in_specs=in_specs, out_specs=out_specs, check_vma=False)
```

time: 695 us -> 116 us (0.17)
  waiting for transfers between devices: 401 us -> 31.1 us
  matrix products: 224 us -> 0 us
  starting transfers between devices: 0.16 us -> 38.3 us
  Pallas kernels: 0 us -> 38.1 us
  loops' own time: 22.1 us -> 0 us
  local copies, waits for them, and re-layouts: 21.7 us -> 4.51 us
  between operations: 13.9 us -> 0.87 us
    reduce_scatter x2 -> x0, waiting for transfers between devices: 237 us -> none  [the longest x1 123 us: local(): lax.psum_scatter(kterms, 'ctx', scatter_dimension=0, tiled=True)]
    dot_general x160 -> x0, matrix products: 224 us -> none  [the longest x32 49.2 us: tile_grads(): jnp.einsum('hqk,kd->qhd', dscore, kblock, precision=highest) * scale]
    all_gather x2 -> x0, waiting for transfers between devices: 162 us -> none  [the longest x1 82.5 us: local(): kpiece = lax.all_gather(key, 'ctx', axis=0, tiled=True)]
    ppermute x0 -> x22, starting transfers between devices: none -> 38.3 us  [send(): return lax.ppermute(x, 'ctx', perm)]
    pallas_call x0 -> x5, Pallas kernels: none -> 38.1 us  [the longest x4 37.9 us: grads(): pl.pallas_call(functools.partial(grads_kernel, offsets, groups, diag, len...]
    ppermute x0 -> x22, waiting for transfers between devices: none -> 31.1 us  [send(): return lax.ppermute(x, 'ctx', perm)]
    another operation x1 -> x0, loops' own time: 22.1 us -> none  [local(): lax.scan(inner, start_q, (kparts, vparts, indices))]
    dynamic_slice x32 -> x0, local copies, waits for them, and re-layouts: 18.6 us -> none  [local(): lax.scan(inner, start_q, (kparts, vparts, indices))]
  transfers between devices with their start and end apart: 4 -> 22, of which waited for: 4 -> 6; matrix products, arithmetic and copies ran while one was open for 0% -> 1% of each run, Pallas kernels for 0% -> 26%
where the time goes in v1:
time: 116 us; the launch traced here: 114 us
  starting transfers between devices  38.3 us (33%)
  Pallas kernels  38.1 us (33%)
  waiting for transfers between devices  31.1 us (27%)
  local copies, waits for them, and re-layouts  4.51 us (4%)
    ppermute x22, starting transfers between devices, send(): return lax.ppermute(x, 'ctx', perm)  38.3 us
    pallas_call x4, Pallas kernels, grads(): pl.pallas_call(functools.partial(grads_kernel, offsets, groups, diag, len...  37.9 us
    ppermute x22, waiting for transfers between devices, send(): return lax.ppermute(x, 'ctx', perm)  31.1 us
    unnamed x15, local copies, waits for them, and re-layouts  3.82 us
  transfers between devices with their start and end apart: 22, of which 6 were waited for; matrix products, arithmetic and copies ran while one was open for 1% of the time, Pallas kernels for 26%

profile of v1, /device:TPU:8, one launch (start us, length us, event | category | flops | bytes accessed | tf_op | source)
XLA Modules:
  0.0 114.0 jit_solution(4850012416445051970)
XLA Ops:
  0.6 1.0 copy-done
  1.7 1.0 copy-done.1
  2.7 1.0 copy-done.2
  3.8 0.7 copy-done.3
  4.5 0.2 pack.1.refs_2_.refs_4_.refs_6_
  4.7 3.1 %collective-permute-start.10 = (f32[128,2176]{1,0:T(8,128)S(1)}, f32[128,2176]{1,0:T(8,128)S(1)}, u32[]{:S(2)}, u32[]{:S(2)}) collective-permute-start(f32[128,2176]{1,0:T(8,128)S(1)} %pack.1.refs_2_.refs_4_.refs_6_), channel_id=1, source_target_pairs={{0,2},{1,3},{2,0},{3,1},{4,6},{5,7},{6,4},{7,5},{8,10},{9,11},{10,... | collective-permute-start | bytes 3342344 | tf_op jit(solution)/shard_map/ppermute | solution.py:30
  7.9 2.0 %collective-permute-start.1 = (f32[128,256]{1,0:T(8,128)S(1)}, f32[128,256]{1,0:T(8,128)S(1)}, u32[]{:S(2)}, u32[]{:S(2)}) collective-permute-start(f32[128,256]{1,0:T(8,128)S(1)} %constant_dynamic-update-slice_fusion.refs_8_), channel_id=1, source_target_pairs={{0,4},{1,5},{2,6},{3,7},{4,8},{5,9},{6,10},{7,11},{8,12},{9,13},{1... | collective-permute-start | bytes 393224 | tf_op jit(solution)/shard_map/ppermute | solution.py:30
  9.8 4.0 %collective-permute-start.4 = (f32[128,256]{1,0:T(8,128)S(1)}, f32[128,256]{1,0:T(8,128)S(1)}, u32[]{:S(2)}, u32[]{:S(2)}) collective-permute-start(f32[128,256]{1,0:T(8,128)S(1)} %constant_dynamic-update-slice_fusion.refs_8_), channel_id=1, source_target_pairs={{0,28},{1,29},{2,30},{3,31},{4,0},{5,1},{6,2},{7,3},{8,4},{9,5},{1... | collective-permute-start | bytes 393224 | tf_op jit(solution)/shard_map/ppermute | solution.py:30
  13.9 4.1 %collective-permute-done.1.refs_9_ = f32[128,256]{1,0:T(8,128)S(1)} collective-permute-done((f32[128,256]{1,0:T(8,128)S(1)}, f32[128,256]{1,0:T(8,128)S(1)}, u32[]{:S(2)}, u32[]{:S(2)}) %collective-permute-start.1) | collective-permute-done | bytes 131104 | tf_op jit(solution)/shard_map/ppermute | solution.py:30
  18.0 3.2 %collective-permute-start.5 = (f32[128,256]{1,0:T(8,128)S(1)}, f32[128,256]{1,0:T(8,128)S(1)}, u32[]{:S(2)}, u32[]{:S(2)}) collective-permute-start(f32[128,256]{1,0:T(8,128)S(1)} %collective-permute-done.4.refs_10_), channel_id=1, source_target_pairs={{0,28},{1,29},{2,30},{3,31},{4,0},{5,1},{6,2},{7,3},{8,4},{9,5},{1... | collective-permute-start | bytes 393224 | tf_op jit(solution)/shard_map/ppermute | solution.py:30
  21.2 3.3 %collective-permute-done.2.refs_11_ = f32[128,256]{1,0:T(8,128)S(1)} collective-permute-done((f32[128,256]{1,0:T(8,128)S(1)}, f32[128,256]{1,0:T(8,128)S(1)}, u32[]{:S(2)}, u32[]{:S(2)}) %collective-permute-start.2) | collective-permute-done | bytes 131104 | tf_op jit(solution)/shard_map/ppermute | solution.py:30
  24.5 0.0 collective-permute-start.3
  24.5 0.0 collective-permute-done.5.refs_12_
  24.5 3.2 %collective-permute-start.6 = (f32[128,256]{1,0:T(8,128)S(1)}, f32[128,256]{1,0:T(8,128)S(1)}, u32[]{:S(2)}, u32[]{:S(2)}) collective-permute-start(f32[128,256]{1,0:T(8,128)S(1)} %collective-permute-done.5.refs_12_), channel_id=1, source_target_pairs={{0,28},{1,29},{2,30},{3,31},{4,0},{5,1},{6,2},{7,3},{8,4},{9,5},{1... | collective-permute-start | bytes 393224 | tf_op jit(solution)/shard_map/ppermute | solution.py:30
  27.7 4.9 %collective-permute-done.10.refs_2_.refs_4_.refs_6_ = f32[128,2176]{1,0:T(8,128)S(1)} collective-permute-done((f32[128,2176]{1,0:T(8,128)S(1)}, f32[128,2176]{1,0:T(8,128)S(1)}, u32[]{:S(2)}, u32[]{:S(2)}) %collective-permute-start.10) | collective-permute-done | bytes 1114144 | tf_op jit(solution)/shard_map/ppermute | solution.py:30
  32.6 0.0 collective-permute-start.11
  32.6 0.0 collective-permute-done.3.refs_8_
  32.6 2.0 %collective-permute-start.7 = (f32[64,256]{1,0:T(8,128)S(1)}, f32[64,256]{1,0:T(8,128)S(1)}, u32[]{:S(2)}, u32[]{:S(2)}) collective-permute-start(f32[64,256]{1,0:T(8,128)S(1)} %slice.64), channel_id=1, source_target_pairs={{0,4},{1,5},{2,6},{3,7},{4,8},{5,9},{6,10},{7,11},{8,12},{9,13},{1... | collective-permute-start | bytes 196616 | tf_op jit(solution)/shard_map/ppermute | solution.py:30
  34.6 0.0 collective-permute-done.6.refs_9_
  34.6 4.0 %collective-permute-start.8 = (f32[64,256]{1,0:T(8,128)S(1)}, f32[64,256]{1,0:T(8,128)S(1)}, u32[]{:S(2)}, u32[]{:S(2)}) collective-permute-start(f32[64,256]{1,0:T(8,128)S(1)} %slice.65), channel_id=1, source_target_pairs={{0,28},{1,29},{2,30},{3,31},{4,0},{5,1},{6,2},{7,3},{8,4},{9,5},{1... | collective-permute-start | bytes 196616 | tf_op jit(solution)/shard_map/ppermute | solution.py:30
  38.7 0.0 collective-permute-done.refs_3_.refs_5_.refs_7_
  38.7 10.6 %grads.4 = (f32[128,1024]{1,0:T(8,128)S(1)}, f32[128,1024]{1,0:T(8,128)S(1)}, f32[128,256]{1,0:T(8,128)S(1)}, f32[128,256]{1,0:T(8,128)S(1)}, f32[128,256]{1,0:T...) custom-call(s32[1]{0:T(128)} %bitcast.refs_0_, s32[64]{0:T(128)S(1)} %copy-done.4, ...), custom_call_target="tpu_custom_call" | custom-call | flops 6710886400 | bytes 2097152 | tf_op jit(solution)/shard_map/grads/pallas_call | solution.py:166
  49.3 0.0 collective-permute-done.7.refs_10_
  49.3 0.0 collective-permute-done.8.refs_11_
  49.3 8.2 %grads.5 = (f32[128,1024]{1,0:T(8,128)S(1)}, f32[128,1024]{1,0:T(8,128)S(1)}, f32[128,256]{1,0:T(8,128)S(1)}, f32[128,256]{1,0:T(8,128)S(1)}, f32[128,256]{1,0:T(8,128)S(1)}) custom-call(s32[1]{0:T(128)} %bitcast.refs_0_, s32[64]{0:T(128)S(1)} %copy-done.4, ...), custom_call_target="tpu_custom_call", output_to_operand_aliasing={{0}: (12, {}), {1}: (13, {})} | custom-call | flops 4026531840 | bytes 2097152 | tf_op jit(solution)/shard_map/grads/pallas_call | solution.py:166
  57.5 0.0 collective-permute-done.11.refs_3_.refs_5_.refs_7_
  57.5 8.1 %grads.6 = (f32[128,1024]{1,0:T(8,128)S(1)}, f32[128,1024]{1,0:T(8,128)S(1)}, f32[128,256]{1,0:T(8,128)S(1)}, f32[128,256]{1,0:T(8,128)S(1)}, f32[128,256]{1,0:T(8,128)S(1)}) custom-call(s32[1]{0:T(128)} %bitcast.refs_0_, s32[64]{0:T(128)S(1)} %copy-done.4, ...), custom_call_target="tpu_custom_call", output_to_operand_aliasing={{2}: (12, {}), {3}: (13, {}), {4}: (14, {})} | custom-call | flops 4026531840 | bytes 2097152 | tf_op jit(solution)/shard_map/grads/pallas_call | solution.py:166
  65.7 0.1 collective-permute-start.14
  65.8 3.2 %collective-permute-start.18 = (f32[64,256]{1,0:T(8,128)S(1)}, f32[64,256]{1,0:T(8,128)S(1)}, u32[]{:S(2)}, u32[]{:S(2)}) collective-permute-start(f32[64,256]{1,0:T(8,128)S(1)} %get-tuple-element.78), channel_id=1, source_target_pairs={{0,28},{1,29},{2,30},{3,31},{4,0},{5,1},{6,2},{7,3},{8,4},{9,5},{1... | collective-permute-start | bytes 196616 | tf_op jit(solution)/shard_map/ppermute | solution.py:30
  69.0 10.9 %grads.7 = (f32[128,1024]{1,0:T(8,128)S(1)}, f32[128,1024]{1,0:T(8,128)S(1)}, f32[128,256]{1,0:T(8,128)S(1)}, f32[128,256]{1,0:T(8,128)S(1)}, f32[128,256]{1,0:T...) custom-call(s32[1]{0:T(128)} %bitcast.refs_0_, ...), custom_call_target="tpu_custom_call", output_to_operand_aliasing={{0}: (13, {}), {1}: (14, {}), {2}: (15, {}), {3}: (16, {}),... | custom-call | flops 6710886400 | bytes 2097152 | tf_op jit(solution)/shard_map/grads/pallas_call | solution.py:166
  79.9 0.1 collective-permute-start.12
  80.0 0.0 collective-permute-done.14
  80.1 0.1 collective-permute-start.15
  80.2 3.3 %collective-permute-start.19 = (f32[128,256]{1,0:T(8,128)S(1)}, f32[128,256]{1,0:T(8,128)S(1)}, u32[]{:S(2)}, u32[]{:S(2)}) collective-permute-start(f32[128,256]{1,0:T(8,128)S(1)} %add_dynamic-update-slice_fusion), channel_id=1, source_target_pairs={{0,28},{1,29},{2,30},{3,31},{4,0},{5,1},{6,2},{7,3},{8,4},{9,5},{1... | collective-permute-start | bytes 393224 | tf_op jit(solution)/shard_map/ppermute | solution.py:30
  83.5 3.8 %collective-permute-done.15 = f32[128,256]{1,0:T(8,128)S(1)} collective-permute-done((f32[128,256]{1,0:T(8,128)S(1)}, f32[128,256]{1,0:T(8,128)S(1)}, u32[]{:S(2)}, u32[]{:S(2)}) %collective-permute-start.15) | collective-permute-done | bytes 131104 | tf_op jit(solution)/shard_map/ppermute | solution.py:30
  87.2 0.1 collective-permute-start.16
  87.4 3.3 %collective-permute-start.20 = (f32[128,256]{1,0:T(8,128)S(1)}, f32[128,256]{1,0:T(8,128)S(1)}, u32[]{:S(2)}, u32[]{:S(2)}) collective-permute-start(f32[128,256]{1,0:T(8,128)S(1)} %add.49), channel_id=1, source_target_pairs={{0,28},{1,29},{2,30},{3,31},{4,0},{5,1},{6,2},{7,3},{8,4},{9,5},{1... | collective-permute-start | bytes 393224 | tf_op jit(solution)/shard_map/ppermute | solution.py:30
  90.7 3.0 %collective-permute-done.16 = f32[128,256]{1,0:T(8,128)S(1)} collective-permute-done((f32[128,256]{1,0:T(8,128)S(1)}, f32[128,256]{1,0:T(8,128)S(1)}, u32[]{:S(2)}, u32[]{:S(2)}) %collective-permute-start.16) | collective-permute-done | bytes 131104 | tf_op jit(solution)/shard_map/ppermute | solution.py:30
  93.7 0.1 collective-permute-start.17
  93.8 0.0 collective-permute-done.20
  93.8 3.3 %collective-permute-start.21 = (f32[128,256]{1,0:T(8,128)S(1)}, f32[128,256]{1,0:T(8,128)S(1)}, u32[]{:S(2)}, u32[]{:S(2)}) collective-permute-start(f32[128,256]{1,0:T(8,128)S(1)} %add.50), channel_id=1, source_target_pairs={{0,28},{1,29},{2,30},{3,31},{4,0},{5,1},{6,2},{7,3},{8,4},{9,5},{1... | collective-permute-start | bytes 393224 | tf_op jit(solution)/shard_map/ppermute | solution.py:30
  97.1 0.0 collective-permute-start.9
  97.1 0.0 collective-permute-done.12
  97.1 0.1 add.42
  97.2 3.1 %collective-permute-start.13 = (f32[128,1024]{1,0:T(8,128)S(1)}, f32[128,1024]{1,0:T(8,128)S(1)}, u32[]{:S(2)}, u32[]{:S(2)}) collective-permute-start(f32[128,1024]{1,0:T(8,128)S(1)} %add.42), channel_id=1, source_target_pairs={{0,2},{1,3},{2,0},{3,1},{4,6},{5,7},{6,4},{7,5},{8,10},{9,11},{10,... | collective-permute-start | bytes 1572872 | tf_op jit(solution)/shard_map/ppermute | solution.py:30
  100.3 0.7 fusion
  101.0 12.1 %collective-permute-done.13 = f32[128,1024]{1,0:T(8,128)S(1)} collective-permute-done((f32[128,1024]{1,0:T(8,128)S(1)}, f32[128,1024]{1,0:T(8,128)S(1)}, u32[]{:S(2)}, u32[]{:S(2)}) %collective-permute-start.13) | collective-permute-done | bytes 524320 | tf_op jit(solution)/shard_map/ppermute | solution.py:30
  113.1 0.9 add_add_fusion
  (30 shorter events, 0.2 us)
Async XLA Ops:
  0.6 1.0 copy-start
  1.7 1.0 copy-start.1
  2.7 1.0 copy-start.2
  3.8 0.7 copy-start.3
  4.4 3.4 %copy-start.5 = (f32[128,128]{1,0:T(8,128)S(1)}, f32[128,128]{1,0:T(8,128)}, u32[]{:S(2)}) copy-start(f32[128,128]{1,0:T(8,128)} %param.12) | copy-start | bytes 196612
  4.4 3.4 %copy-start.6 = (f32[128,128]{1,0:T(8,128)S(1)}, f32[128,128]{1,0:T(8,128)}, u32[]{:S(2)}) copy-start(f32[128,128]{1,0:T(8,128)} %param.13) | copy-start | bytes 196612
  4.5 34.2 %copy-start.4 = (s32[64]{0:T(128)S(1)}, s32[64]{0:T(128)}, u32[]{:S(2)}) copy-start(s32[64]{0:T(128)} %refs_1_.7) | copy-start | bytes 772
  4.7 27.9 %collective-permute-start.10 = (f32[128,2176]{1,0:T(8,128)S(1)}, f32[128,2176]{1,0:T(8,128)S(1)}, u32[]{:S(2)}, u32[]{:S(2)}) collective-permute-start(f32[128,2176]{1,0:T(8,128)S(1)} %pack.1.refs_2_.refs_4_.refs_6_), channel_id=1, source_target_pairs={{0,2},{1,3},{2,0},{3,1},{4,6},{5,7},{6,4},{7,5},{8,10},{9,11},{10,... | collective-permute-start | bytes 3342344 | tf_op jit(solution)/shard_map/ppermute | solution.py:30
  7.8 30.8 %collective-permute-start = (f32[128,2176]{1,0:T(8,128)S(1)}, f32[128,2176]{1,0:T(8,128)}, u32[]{:S(2)}, u32[]{:S(2)}) collective-permute-start(f32[128,2176]{1,0:T(8,128)S(1)} %pack.1.refs_2_.refs_4_.refs_6_), channel_id=1, source_target_pairs={{0,1},{1,0},{2,3},{3,2},{4,5},{5,4},{6,7},{7,6},{8,9},{9,8},{10,11... | collective-permute-start | bytes 3342344 | tf_op jit(solution)/shard_map/ppermute | solution.py:30
  7.9 10.1 %collective-permute-start.1 = (f32[128,256]{1,0:T(8,128)S(1)}, f32[128,256]{1,0:T(8,128)S(1)}, u32[]{:S(2)}, u32[]{:S(2)}) collective-permute-start(f32[128,256]{1,0:T(8,128)S(1)} %constant_dynamic-update-slice_fusion.refs_8_), channel_id=1, source_target_pairs={{0,4},{1,5},{2,6},{3,7},{4,8},{5,9},{6,10},{7,11},{8,12},{9,13},{1... | collective-permute-start | bytes 393224 | tf_op jit(solution)/shard_map/ppermute | solution.py:30
  9.8 8.1 %collective-permute-start.4 = (f32[128,256]{1,0:T(8,128)S(1)}, f32[128,256]{1,0:T(8,128)S(1)}, u32[]{:S(2)}, u32[]{:S(2)}) collective-permute-start(f32[128,256]{1,0:T(8,128)S(1)} %constant_dynamic-update-slice_fusion.refs_8_), channel_id=1, source_target_pairs={{0,28},{1,29},{2,30},{3,31},{4,0},{5,1},{6,2},{7,3},{8,4},{9,5},{1... | collective-permute-start | bytes 393224 | tf_op jit(solution)/shard_map/ppermute | solution.py:30
  18.0 6.5 %collective-permute-start.2 = (f32[128,256]{1,0:T(8,128)S(1)}, f32[128,256]{1,0:T(8,128)S(1)}, u32[]{:S(2)}, u32[]{:S(2)}) collective-permute-start(f32[128,256]{1,0:T(8,128)S(1)} %collective-permute-done.1.refs_9_), channel_id=1, source_target_pairs={{0,4},{1,5},{2,6},{3,7},{4,8},{5,9},{6,10},{7,11},{8,12},{9,13},{1... | collective-permute-start | bytes 393224 | tf_op jit(solution)/shard_map/ppermute | solution.py:30
  18.0 6.5 %collective-permute-start.5 = (f32[128,256]{1,0:T(8,128)S(1)}, f32[128,256]{1,0:T(8,128)S(1)}, u32[]{:S(2)}, u32[]{:S(2)}) collective-permute-start(f32[128,256]{1,0:T(8,128)S(1)} %collective-permute-done.4.refs_10_), channel_id=1, source_target_pairs={{0,28},{1,29},{2,30},{3,31},{4,0},{5,1},{6,2},{7,3},{8,4},{9,5},{1... | collective-permute-start | bytes 393224 | tf_op jit(solution)/shard_map/ppermute | solution.py:30
  24.5 8.1 %collective-permute-start.3 = (f32[128,256]{1,0:T(8,128)S(1)}, f32[128,256]{1,0:T(8,128)S(1)}, u32[]{:S(2)}, u32[]{:S(2)}) collective-permute-start(f32[128,256]{1,0:T(8,128)S(1)} %collective-permute-done.2.refs_11_), channel_id=1, source_target_pairs={{0,4},{1,5},{2,6},{3,7},{4,8},{5,9},{6,10},{7,11},{8,12},{9,13},{1... | collective-permute-start | bytes 393224 | tf_op jit(solution)/shard_map/ppermute | solution.py:30
  24.5 10.1 %collective-permute-start.6 = (f32[128,256]{1,0:T(8,128)S(1)}, f32[128,256]{1,0:T(8,128)S(1)}, u32[]{:S(2)}, u32[]{:S(2)}) collective-permute-start(f32[128,256]{1,0:T(8,128)S(1)} %collective-permute-done.5.refs_12_), channel_id=1, source_target_pairs={{0,28},{1,29},{2,30},{3,31},{4,0},{5,1},{6,2},{7,3},{8,4},{9,5},{1... | collective-permute-start | bytes 393224 | tf_op jit(solution)/shard_map/ppermute | solution.py:30
  32.6 24.9 %collective-permute-start.11 = (f32[128,2176]{1,0:T(8,128)S(1)}, f32[128,2176]{1,0:T(8,128)}, u32[]{:S(2)}, u32[]{:S(2)}) collective-permute-start(f32[128,2176]{1,0:T(8,128)S(1)} %collective-permute-done.10.refs_2_.refs_4_.refs_6_), channel_id=1, source_target_pairs={{0,1},{1,0},{2,3},{3,2},{4,5},{5,4},{6,7},{7,6},{8,9},{9,8},{10,11... | collective-permute-start | bytes 3342344 | tf_op jit(solution)/shard_map/ppermute | solution.py:30
  32.6 16.7 %collective-permute-start.7 = (f32[64,256]{1,0:T(8,128)S(1)}, f32[64,256]{1,0:T(8,128)S(1)}, u32[]{:S(2)}, u32[]{:S(2)}) collective-permute-start(f32[64,256]{1,0:T(8,128)S(1)} %slice.64), channel_id=1, source_target_pairs={{0,4},{1,5},{2,6},{3,7},{4,8},{5,9},{6,10},{7,11},{8,12},{9,13},{1... | collective-permute-start | bytes 196616 | tf_op jit(solution)/shard_map/ppermute | solution.py:30
  34.6 14.7 %collective-permute-start.8 = (f32[64,256]{1,0:T(8,128)S(1)}, f32[64,256]{1,0:T(8,128)S(1)}, u32[]{:S(2)}, u32[]{:S(2)}) collective-permute-start(f32[64,256]{1,0:T(8,128)S(1)} %slice.65), channel_id=1, source_target_pairs={{0,28},{1,29},{2,30},{3,31},{4,0},{5,1},{6,2},{7,3},{8,4},{9,5},{1... | collective-permute-start | bytes 196616 | tf_op jit(solution)/shard_map/ppermute | solution.py:30
  65.7 14.4 %collective-permute-start.14 = (f32[64,256]{1,0:T(8,128)S(1)}, f32[64,256]{1,0:T(8,128)S(1)}, u32[]{:S(2)}, u32[]{:S(2)}) collective-permute-start(f32[64,256]{1,0:T(8,128)S(1)} %get-tuple-element.77), channel_id=1, source_target_pairs={{0,4},{1,5},{2,6},{3,7},{4,8},{5,9},{6,10},{7,11},{8,12},{9,13},{1... | collective-permute-start | bytes 196616 | tf_op jit(solution)/shard_map/ppermute | solution.py:30
  65.8 14.4 %collective-permute-start.18 = (f32[64,256]{1,0:T(8,128)S(1)}, f32[64,256]{1,0:T(8,128)S(1)}, u32[]{:S(2)}, u32[]{:S(2)}) collective-permute-start(f32[64,256]{1,0:T(8,128)S(1)} %get-tuple-element.78), channel_id=1, source_target_pairs={{0,28},{1,29},{2,30},{3,31},{4,0},{5,1},{6,2},{7,3},{8,4},{9,5},{1... | collective-permute-start | bytes 196616 | tf_op jit(solution)/shard_map/ppermute | solution.py:30
  79.9 17.2 %collective-permute-start.12 = (f32[128,1024]{1,0:T(8,128)S(1)}, f32[128,1024]{1,0:T(8,128)S(1)}, u32[]{:S(2)}, u32[]{:S(2)}) collective-permute-start(f32[128,1024]{1,0:T(8,128)S(1)} %get-tuple-element.66), channel_id=1, source_target_pairs={{0,1},{1,0},{2,3},{3,2},{4,5},{5,4},{6,7},{7,6},{8,9},{9,8},{10,11... | collective-permute-start | bytes 1572872 | tf_op jit(solution)/shard_map/ppermute | solution.py:30
  80.1 7.2 %collective-permute-start.15 = (f32[128,256]{1,0:T(8,128)S(1)}, f32[128,256]{1,0:T(8,128)S(1)}, u32[]{:S(2)}, u32[]{:S(2)}) collective-permute-start(f32[128,256]{1,0:T(8,128)S(1)} %add_dynamic-update-slice_fusion.1), channel_id=1, source_target_pairs={{0,4},{1,5},{2,6},{3,7},{4,8},{5,9},{6,10},{7,11},{8,12},{9,13},{1... | collective-permute-start | bytes 393224 | tf_op jit(solution)/shard_map/ppermute | solution.py:30
  80.2 7.2 %collective-permute-start.19 = (f32[128,256]{1,0:T(8,128)S(1)}, f32[128,256]{1,0:T(8,128)S(1)}, u32[]{:S(2)}, u32[]{:S(2)}) collective-permute-start(f32[128,256]{1,0:T(8,128)S(1)} %add_dynamic-update-slice_fusion), channel_id=1, source_target_pairs={{0,28},{1,29},{2,30},{3,31},{4,0},{5,1},{6,2},{7,3},{8,4},{9,5},{1... | collective-permute-start | bytes 393224 | tf_op jit(solution)/shard_map/ppermute | solution.py:30
  87.2 6.4 %collective-permute-start.16 = (f32[128,256]{1,0:T(8,128)S(1)}, f32[128,256]{1,0:T(8,128)S(1)}, u32[]{:S(2)}, u32[]{:S(2)}) collective-permute-start(f32[128,256]{1,0:T(8,128)S(1)} %add.45), channel_id=1, source_target_pairs={{0,4},{1,5},{2,6},{3,7},{4,8},{5,9},{6,10},{7,11},{8,12},{9,13},{1... | collective-permute-start | bytes 393224 | tf_op jit(solution)/shard_map/ppermute | solution.py:30
  87.4 6.4 %collective-permute-start.20 = (f32[128,256]{1,0:T(8,128)S(1)}, f32[128,256]{1,0:T(8,128)S(1)}, u32[]{:S(2)}, u32[]{:S(2)}) collective-permute-start(f32[128,256]{1,0:T(8,128)S(1)} %add.49), channel_id=1, source_target_pairs={{0,28},{1,29},{2,30},{3,31},{4,0},{5,1},{6,2},{7,3},{8,4},{9,5},{1... | collective-permute-start | bytes 393224 | tf_op jit(solution)/shard_map/ppermute | solution.py:30
  93.7 6.6 %collective-permute-start.17 = (f32[128,256]{1,0:T(8,128)S(1)}, f32[128,256]{1,0:T(8,128)S(1)}, u32[]{:S(2)}, u32[]{:S(2)}) collective-permute-start(f32[128,256]{1,0:T(8,128)S(1)} %add.46), channel_id=1, source_target_pairs={{0,4},{1,5},{2,6},{3,7},{4,8},{5,9},{6,10},{7,11},{8,12},{9,13},{1... | collective-permute-start | bytes 393224 | tf_op jit(solution)/shard_map/ppermute | solution.py:30
  93.8 6.5 %collective-permute-start.21 = (f32[128,256]{1,0:T(8,128)S(1)}, f32[128,256]{1,0:T(8,128)S(1)}, u32[]{:S(2)}, u32[]{:S(2)}) collective-permute-start(f32[128,256]{1,0:T(8,128)S(1)} %add.50), channel_id=1, source_target_pairs={{0,28},{1,29},{2,30},{3,31},{4,0},{5,1},{6,2},{7,3},{8,4},{9,5},{1... | collective-permute-start | bytes 393224 | tf_op jit(solution)/shard_map/ppermute | solution.py:30
  97.1 3.9 %collective-permute-start.9 = (f32[128,1024]{1,0:T(8,128)S(1)}, f32[128,1024]{1,0:T(8,128)S(1)}, u32[]{:S(2)}, u32[]{:S(2)}) collective-permute-start(f32[128,1024]{1,0:T(8,128)S(1)} %get-tuple-element.54), channel_id=1, source_target_pairs={{0,1},{1,0},{2,3},{3,2},{4,5},{5,4},{6,7},{7,6},{8,9},{9,8},{10,11... | collective-permute-start | bytes 1572872 | tf_op jit(solution)/shard_map/ppermute | solution.py:30
  97.2 15.9 %collective-permute-start.13 = (f32[128,1024]{1,0:T(8,128)S(1)}, f32[128,1024]{1,0:T(8,128)S(1)}, u32[]{:S(2)}, u32[]{:S(2)}) collective-permute-start(f32[128,1024]{1,0:T(8,128)S(1)} %add.42), channel_id=1, source_target_pairs={{0,2},{1,3},{2,0},{3,1},{4,6},{5,7},{6,4},{7,5},{8,10},{9,11},{10,... | collective-permute-start | bytes 1572872 | tf_op jit(solution)/shard_map/ppermute | solution.py:30
